TPU v7x, 256 devices: a whole 4x4x8 slice. The times are simulated.
256 devices in a mesh: dp: 8 (over z), expert: 32 (over x, y, core).
Axes of the slice: x: 4, y: 4, z: 8, core: 2. Of those that a mesh axis runs over, the one named last changes fastest.
Arguments:
- tokens: bfloat16 [12288, 2048], P(('dp', 'expert')), may hold values from -6 to 6
- tokens_dot: bfloat16 [12288, 2048], P(('dp', 'expert')), may hold values from -6 to 6
- router: bfloat16 [2048, 64], replicated, may hold values from -0.125 to 0.125
- router_dot: bfloat16 [2048, 64], replicated, may hold values from -0.125 to 0.125
- expert_ids: int32 [12288, 8], P(('dp', 'expert')), may hold values from 0 to 63, all different within a row; in each aligned block of 48 rows (0 to 47, 48 to 95, ...) at most 12 rows name the same one
- priority: int32 [12288], P(('dp', 'expert')), may hold values from 0 to 12287, each once
- w_gate: bfloat16 [64, 768, 2048], P('expert', 'dp'), may hold values from -0.125 to 0.125
- w_up: bfloat16 [64, 768, 2048], P('expert', 'dp'), may hold values from -0.125 to 0.125
- w_down: bfloat16 [64, 768, 2048], P('expert', 'dp'), may hold values from -0.21875 to 0.21875
Outputs:
- mixed: bfloat16 [12288, 2048], P(('dp', 'expert'))
- mixed_dot: bfloat16 [12288, 2048], P(('dp', 'expert'))
Inputs may be any that keep to these rules, and one draw needn't show every extreme that they name: `expert_ids`: each token names 8 different experts; among the tokens of one device no expert is named more than 12 times, and exactly 12 times in some device. `priority`: each rank appears once.
All inputs are finite; a program needn't handle non-finite values.
Results may differ from a plain program's by a relative error of at most 0.0058.
Values may be sent and summed in bfloat16 or wider, within the bound.
A program may use at most 128 MiB of HBM per device.

v0:
```python
import jax
import jax.numpy as jnp
from jax import lax
from jax.sharding import PartitionSpec as P

TOP = 8
MOST = 12
CAP = 192


def hidden_units(stacked, gate_piece, up_piece):
    gate_all = jnp.einsum("ercd,efd->ercf", stacked, gate_piece, preferred_element_type=jnp.float32)
    up_all = jnp.einsum("ercd,efd->ercf", stacked, up_piece, preferred_element_type=jnp.float32)
    gate_p = gate_all[:, 0]
    up_p = up_all[:, 0]
    sigma = 1.0 / (1.0 + jnp.exp(-gate_p))
    act = gate_p * sigma * up_p
    act_dot = (
        sigma * (1.0 + gate_p * (1.0 - sigma)) * gate_all[:, 1] * up_p
        + gate_p * sigma * up_all[:, 1]
    )
    return jnp.stack([act, act_dot], axis=1).astype(jnp.bfloat16)


def shards(tokens, tokens_dot, router, router_dot, expert_ids, priority, w_gate, w_up, w_down):
    tok_count = tokens.shape[0]
    feat_width = tokens.shape[1]
    expert_count = router.shape[1]
    local_count = w_gate.shape[0]
    peer_count = lax.axis_size("expert")
    slot_count = MOST
    sentinel = 2**30
    member = (
        expert_ids[:, :, None] == jnp.arange(expert_count, dtype=jnp.int32)[None, None, :]
    ).astype(jnp.int32)
    member_flat = member.reshape(tok_count * TOP, expert_count)
    before = jnp.cumsum(member_flat, axis=0) - member_flat
    slot_index = jnp.sum(before * member_flat, axis=1)
    target = expert_ids.reshape(-1) * slot_count + slot_index
    owner_tok = jnp.arange(tok_count * TOP, dtype=jnp.int32) // TOP
    joined = jnp.concatenate([tokens, tokens_dot], axis=1)
    outgoing = (
        jnp.zeros((expert_count * slot_count, 2 * feat_width), jnp.bfloat16)
        .at[target]
        .set(joined[owner_tok])
    )
    out_ranks = (
        jnp.full((expert_count * slot_count,), sentinel, jnp.int32)
        .at[target]
        .set(priority[owner_tok])
    )
    outgoing = outgoing.reshape(peer_count, local_count * slot_count, 2 * feat_width)
    out_ranks = out_ranks.reshape(peer_count, local_count * slot_count)
    arrived, arrived_rank = (
        lax.all_to_all(outgoing, "expert", split_axis=0, concat_axis=0, tiled=True),
        lax.all_to_all(out_ranks, "expert", split_axis=0, concat_axis=0, tiled=True),
    )
    arrived = arrived.reshape(peer_count, local_count, slot_count, 2, feat_width)
    rank_local = jnp.transpose(
        arrived_rank.reshape(peer_count, local_count, slot_count), (1, 0, 2)
    ).reshape(local_count, peer_count * slot_count)
    usable = rank_local < sentinel
    ahead = jnp.sum(
        (usable[:, None, :] & (rank_local[:, None, :] < rank_local[:, :, None])).astype(jnp.int32),
        axis=2,
    )
    kept = usable & (ahead < CAP)
    placing = (
        kept[:, None, :] & (ahead[:, None, :] == jnp.arange(CAP, dtype=jnp.int32)[None, :, None])
    ).astype(jnp.bfloat16)
    placing = placing.reshape(local_count, CAP, peer_count, slot_count)
    packed = jnp.einsum(
        "ecsm,semrd->ercd", placing, arrived, preferred_element_type=jnp.float32
    ).astype(jnp.bfloat16)
    gate_piece = lax.all_gather(w_gate, "dp", axis=1, tiled=True)
    up_piece = lax.all_gather(w_up, "dp", axis=1, tiled=True)
    down_piece = lax.all_gather(w_down, "dp", axis=1, tiled=True)
    hidden = hidden_units(packed, gate_piece, up_piece)
    expert_out = jnp.einsum(
        "ercf,efd->ercd", hidden, down_piece, preferred_element_type=jnp.float32
    )
    out_bf = expert_out.astype(jnp.bfloat16)
    returning = jnp.einsum(
        "ecsm,ercd->semrd", placing, out_bf, preferred_element_type=jnp.float32
    ).astype(jnp.bfloat16)
    returning = returning.reshape(peer_count, local_count * slot_count, 2 * feat_width)
    landed = lax.all_to_all(returning, "expert", split_axis=0, concat_axis=0, tiled=True)
    landed = landed.reshape(expert_count * slot_count, 2, feat_width)
    results = landed[target].reshape(tok_count, TOP, 2, feat_width).astype(jnp.float32)
    logits = jnp.dot(tokens, router, preferred_element_type=jnp.float32)
    logits_dot = jnp.dot(tokens_dot, router, preferred_element_type=jnp.float32) + jnp.dot(
        tokens, router_dot, preferred_element_type=jnp.float32
    )
    member_f = member.astype(jnp.float32)
    chosen = jnp.sum(member_f * logits[:, None, :], axis=2)
    chosen_dot = jnp.sum(member_f * logits_dot[:, None, :], axis=2)
    expo = jnp.exp(chosen)
    gates = expo / jnp.sum(expo, axis=1, keepdims=True)
    gates_dot = gates * (chosen_dot - jnp.sum(gates * chosen_dot, axis=1, keepdims=True))
    mixed = jnp.sum(gates[:, :, None] * results[:, :, 0], axis=1)
    mixed_dot = jnp.sum(
        gates_dot[:, :, None] * results[:, :, 0] + gates[:, :, None] * results[:, :, 1], axis=1
    )
    return (mixed.astype(jnp.bfloat16), mixed_dot.astype(jnp.bfloat16))


def solution(mesh):
    return jax.shard_map(
        shards,
        mesh=mesh,
        in_specs=(
            P(("dp", "expert"), None),
            P(("dp", "expert"), None),
            P(),
            P(),
            P(("dp", "expert"), None),
            P(("dp", "expert")),
            P("expert", "dp", None),
            P("expert", "dp", None),
            P("expert", "dp", None),
        ),
        out_specs=(P(("dp", "expert"), None), P(("dp", "expert"), None)),
        check_vma=False,
    )
```

profile of v0, /device:TPU:8, one launch (start us, length us, event | category | flops | bytes accessed | tf_op | source)
XLA Modules:
  0.0 415.2 jit_solution(13426487562719504342)
XLA Ops:
  7.2 0.7 all-gather.4.cloned.1.call-update
  8.0 0.7 all-gather.6.cloned.1.call-update
  8.7 0.7 all-gather.8.cloned.1.call-update
  9.4 0.8 copy.37
  10.2 0.1 eq.53
  10.3 0.1 eq.49
  10.4 0.9 reduce-window.6
  11.3 0.2 slice_reduce_fusion
  11.6 0.7 broadcast_multiply_fusion
  12.3 0.1 mul.102
  12.5 0.1 fusion.38
  12.6 1.7 fusion.48
  14.3 2.1 fusion.46
  16.4 2.1 fusion.47
  18.5 30.2 %select_select_fusion = s32[384]{0:T(512)S(1)} fusion(s32[384]{0:T(512)S(1)} %fusion.43, s32[]{:T(128)} %bitcast.2, s32[]{:T(128)} %bitcast.3, s32[]{:T(128)} %bitcast.4, s32[]{:T(128)} %bitcast.5, s32[]{:T(128)} %bitcast.6, s32[]{:T(128)} %bitcast.7, s32[]{:T(128)} %bitcast.8, s32[]{:T(128)} %bitcast.9, s32[]{:T(128)} %bitcast.10, s32[]{:T(128)} %bitcast.11, ...), kind=kLoop, calls=%fused_computation.72 | loop fusion | flops 36096 | bytes 3264 | tf_op jit(solution)/shard_map/gather | solution.py:50
  48.7 2.9 scatter_custom_fusion.1
  51.6 0.7 all_to_all.13
  52.3 8.2 %all-to-all-start.1 = ((s32[32,1,24]{2,1,0:T(1,128)}), s32[32,1,24]{2,1,0:T(1,128)S(1)}, u32[]{:S(2)}, u32[]{:S(2)}) async-start(s32[32,1,24]{2,1,0:T(1,128)} %bitcast.50), calls=%async_computation.1 | async-start | bytes 32768 | tf_op jit(solution)/shard_map/all_to_all | solution.py:56
  60.5 17.9 %scatter_custom_fusion = bf16[768,4096]{1,0:T(8,128)(2,1)} fusion(s32[384]{0:T(512)S(1)} %fusion.42, bf16[48,4096]{1,0:T(8,128)(2,1)S(1)} %pad_maximum_fusion, s32[1024]{0:T(1024)S(1)} %pad_clamp_fusion.1, bf16[]{:T(256)} %constant.15.clone.1), kind=kCustom, calls=%fused_computation.22 | custom fusion | bytes 6291458 | tf_op jit(solution)/shard_map/scatter | solution.py:45
  78.4 7.4 %all-to-all-start = ((bf16[32,24,4096]{2,1,0:T(8,128)(2,1)}), bf16[32,24,4096]{2,1,0:T(8,128)(2,1)}, u32[]{:S(2)}, u32[]{:S(2)}) async-start(bf16[32,24,4096]{2,1,0:T(8,128)(2,1)} %bitcast.133), calls=%async_computation | async-start | bytes 12582912 | tf_op jit(solution)/shard_map/all_to_all | solution.py:55
  85.9 0.1 copy.44
  86.0 0.1 reshape.198
  86.1 0.3 convert_reduce_fusion
  86.5 0.1 reduce_sum.81
  86.6 0.1 copy.45
  86.7 86.7 %all-to-all-done = bf16[32,24,4096]{2,1,0:T(8,128)(2,1)} async-done(((bf16[32,24,4096]{2,1,0:T(8,128)(2,1)}), bf16[32,24,4096]{2,1,0:T(8,128)(2,1)}, u32[]{:S(2)}, u32[]{:S(2)}) %all-to-all-start) | async-done | bytes 6291488 | tf_op jit(solution)/shard_map/all_to_all | solution.py:55
  173.4 11.5 %reshape.196 = bf16[32,2,12,2,2048]{4,3,2,1,0:T(2,128)(2,1)} reshape(bf16[32,24,4096]{2,1,0:T(8,128)(2,1)} %all-to-all-done) | data formatting | bytes 12582912 | tf_op jit(solution)/shard_map/reshape | solution.py:58
  184.9 8.9 %bitcast_convert_fusion = bf16[2,2,2048,192]{2,3,1,0:T(8,128)(2,1)} fusion(bf16[32,2,12,2,2048]{4,3,2,1,0:T(2,128)(2,1)} %reshape.196, s32[2,32,12]{1,2,0:T(8,128)S(1)} %copy.45, pred[2,32,12]{1,2,0:T(8,128)(4,1)S(1)} %compare_and_fusion), kind=kOutput, calls=%fused_computation.10 | convolution fusion | flops 1209827328 | bytes 9441024 | tf_op jit(solution)/shard_map/ecsm,semrd->ercd/dot_general | solution.py:72
  193.8 6.4 %fusion.4 = f32[2,2,192,768]{3,2,1,0:T(8,128)S(1)} fusion(bf16[2,768,2048]{2,1,0:T(8,128)(2,1)} %all-gather.4.cloned.1.call-done, bf16[2,2,2048,192]{2,3,1,0:T(8,128)(2,1)} %bitcast_convert_fusion), kind=kOutput, calls=%fused_computation.8 | convolution fusion | flops 2415919104 | bytes 11796480 | tf_op jit(solution)/shard_map/ercd,efd->ercf/dot_general | solution.py:12
  200.3 6.4 %fusion.2 = f32[2,2,192,768]{3,2,1,0:T(8,128)S(1)} fusion(bf16[2,768,2048]{2,1,0:T(8,128)(2,1)} %all-gather.6.cloned.1.call-done, bf16[2,2,2048,192]{2,3,1,0:T(8,128)(2,1)} %bitcast_convert_fusion), kind=kOutput, calls=%fused_computation.6 | convolution fusion | flops 2415919104 | bytes 11796480 | tf_op jit(solution)/shard_map/ercd,efd->ercf/dot_general | solution.py:13
  206.7 1.7 multiply_convert_fusion
  208.4 28.7 %all-gather.8.cloned.1.call-done = bf16[2,768,2048]{2,1,0:T(8,128)(2,1)} async-done(((bf16[2,96,2048]{2,1,0:T(8,128)(2,1)}), bf16[2,768,2048]{2,1,0:T(8,128)(2,1)}) %all-gather.8.cloned.1.call-update) | async-done | bytes 6291472 | tf_op jit(solution)/shard_map/all_gather | solution.py:77
  237.1 5.8 %fusion.10 = bf16[2,2,192,2048]{3,2,1,0:T(8,128)(2,1)S(1)} fusion(bf16[2,768,2048]{2,1,0:T(8,128)(2,1)} %all-gather.8.cloned.1.call-done, bf16[2,1,192,768]{3,2,1,0:T(8,128)(2,1)} %get-tuple-element.9, bf16[2,1,192,768]{3,2,1,0:T(8,128)(2,1)} %get-tuple-element.8), kind=kOutput, calls=%fused_computation.14 | convolution fusion | flops 2418081792 | bytes 10616832 | tf_op jit(solution)/shard_map/ercf,efd->ercd/dot_general | solution.py:79
  242.8 2.5 convert_bitcast_fusion
  245.4 14.0 %copy.48 = bf16[32,2,12,2,2048]{4,3,2,1,0:T(2,128)(2,1)} copy(bf16[32,2,12,2,2048]{4,0,2,3,1:T(8,128)(2,1)S(1)} %convert_bitcast_fusion) | data formatting | bytes 12582912 | tf_op jit(solution)/shard_map/convert_element_type | solution.py:85
  259.4 11.1 %reshape.199 = bf16[32,24,4096]{2,1,0:T(8,128)(2,1)} reshape(bf16[32,2,12,2,2048]{4,3,2,1,0:T(2,128)(2,1)} %copy.48) | data formatting | bytes 12582912 | tf_op jit(solution)/shard_map/reshape | solution.py:86
  270.5 7.6 %all-to-all-start.2 = ((bf16[32,24,4096]{2,1,0:T(8,128)(2,1)}), bf16[32,24,4096]{2,1,0:T(8,128)(2,1)}, u32[]{:S(2)}, u32[]{:S(2)}) async-start(bf16[32,24,4096]{2,1,0:T(8,128)(2,1)} %reshape.199), calls=%async_computation.2 | async-start | bytes 12582912 | tf_op jit(solution)/shard_map/all_to_all | solution.py:87
  278.1 0.2 fusion.50
  278.3 0.2 fusion.49
  278.5 0.2 convolution_add_fusion
  278.7 0.2 multiply_reduce_fusion.1
  279.0 0.1 exponential_reduce_fusion
  279.1 0.2 multiply_reduce_fusion.3
  279.4 86.3 %all-to-all-done.2 = bf16[32,24,4096]{2,1,0:T(8,128)(2,1)} async-done(((bf16[32,24,4096]{2,1,0:T(8,128)(2,1)}), bf16[32,24,4096]{2,1,0:T(8,128)(2,1)}, u32[]{:S(2)}, u32[]{:S(2)}) %all-to-all-start.2) | async-done | bytes 6291488 | tf_op jit(solution)/shard_map/all_to_all | solution.py:87
  365.6 11.1 %reshape.200 = bf16[768,2,2048]{2,1,0:T(2,128)(2,1)} reshape(bf16[32,24,4096]{2,1,0:T(8,128)(2,1)} %all-to-all-done.2) | data formatting | bytes 12582912 | tf_op jit(solution)/shard_map/reshape | solution.py:88
  376.8 17.7 %gather_fusion = bf16[384,2,2048]{2,1,0:T(2,128)(2,1)S(1)} fusion(bf16[768,2,2048]{2,1,0:T(2,128)(2,1)} %reshape.200, s32[1024]{0:T(1024)S(1)} %pad_clamp_fusion), kind=kCustom, calls=%fused_computation.1 | custom fusion | bytes 6292992 | tf_op jit(solution)/shard_map/gather | solution.py:89
  394.5 6.5 %fusion.45 = (f32[48,8,1,2048]{3,2,1,0:T(1,128)S(1)}, f32[48,8,1,2048]{3,2,1,0:T(1,128)}) fusion(bf16[48,8,2,2048]{3,2,1,0:T(2,128)(2,1)S(1)} %bitcast.132), kind=kLoop, calls=%fused_computation.80 | loop fusion | bytes 12582912 | tf_op jit(solution)/shard_map/slice | solution.py:100
  401.0 7.5 %fusion.14 = (bf16[48,2048]{1,0:T(8,128)(2,1)}, bf16[48,2048]{1,0:T(8,128)(2,1)}) fusion(f32[48,8,1,2048]{3,2,1,0:T(1,128)} %get-tuple-element.11, f32[48,8,1,2048]{3,2,1,0:T(1,128)S(1)} %get-tuple-element.10, f32[48,8]{1,0:T(8,128)S(1)} %subtract_multiply_fusion, f32[48,8]{1,0:T(8,128)S(1)} %get-tuple-element.7), kind=kLoop, calls=%fused_computation.18 | loop fusion | flops 4521984 | bytes 6687744 | tf_op jit(solution)/shard_map/reduce_sum | solution.py:101
  (27 shorter events, 0.6 us)
Async XLA Ops:
  7.2 270.9 %copy-start = (bf16[2048,64]{0,1:T(8,128)(2,1)S(1)}, bf16[2048,64]{0,1:T(8,128)(2,1)}, u32[]{:S(2)}) copy-start(bf16[2048,64]{0,1:T(8,128)(2,1)} %param.11) | copy-start | bytes 786436
  7.2 53.3 %copy-start.2 = (bf16[48,2048]{1,0:T(8,128)(2,1)S(1)}, bf16[48,2048]{1,0:T(8,128)(2,1)}, u32[]{:S(2)}) copy-start(bf16[48,2048]{1,0:T(8,128)(2,1)} %param.10) | copy-start | bytes 589828
  7.2 53.3 %copy-start.1 = (bf16[48,2048]{1,0:T(8,128)(2,1)S(1)}, bf16[48,2048]{1,0:T(8,128)(2,1)}, u32[]{:S(2)}) copy-start(bf16[48,2048]{1,0:T(8,128)(2,1)} %param.9) | copy-start | bytes 589828
  7.2 186.6 %all-gather.4.cloned.1.call-start = ((), (), s32[]{:S(2)}) async-start(), calls=%async_computation.3 | async-start | bytes 7077888 | tf_op jit(solution)/shard_map/all_gather | solution.py:75
  7.9 192.3 %all-gather.6.cloned.1.call-start = ((), (), s32[]{:S(2)}) async-start(), calls=%async_computation.4 | async-start | bytes 7077888 | tf_op jit(solution)/shard_map/all_gather | solution.py:76
  8.7 228.4 %all-gather.8.cloned.1.call-start = ((), (), s32[]{:S(2)}) async-start(), calls=%async_computation.5 | async-start | bytes 7077888 | tf_op jit(solution)/shard_map/all_gather | solution.py:77
  52.3 26.1 %all-to-all-start.1 = ((s32[32,1,24]{2,1,0:T(1,128)}), s32[32,1,24]{2,1,0:T(1,128)S(1)}, u32[]{:S(2)}, u32[]{:S(2)}) async-start(s32[32,1,24]{2,1,0:T(1,128)} %bitcast.50), calls=%async_computation.1 | async-start | bytes 32768 | tf_op jit(solution)/shard_map/all_to_all | solution.py:56
  78.4 95.0 %all-to-all-start = ((bf16[32,24,4096]{2,1,0:T(8,128)(2,1)}), bf16[32,24,4096]{2,1,0:T(8,128)(2,1)}, u32[]{:S(2)}, u32[]{:S(2)}) async-start(bf16[32,24,4096]{2,1,0:T(8,128)(2,1)} %bitcast.133), calls=%async_computation | async-start | bytes 12582912 | tf_op jit(solution)/shard_map/all_to_all | solution.py:55
  270.5 8.0 %copy-start.3 = (bf16[2048,64]{0,1:T(8,128)(2,1)S(1)}, bf16[2048,64]{0,1:T(8,128)(2,1)}, u32[]{:S(2)}) copy-start(bf16[2048,64]{0,1:T(8,128)(2,1)} %param.12) | copy-start | bytes 786436
  270.5 95.2 %all-to-all-start.2 = ((bf16[32,24,4096]{2,1,0:T(8,128)(2,1)}), bf16[32,24,4096]{2,1,0:T(8,128)(2,1)}, u32[]{:S(2)}, u32[]{:S(2)}) async-start(bf16[32,24,4096]{2,1,0:T(8,128)(2,1)} %reshape.199), calls=%async_computation.2 | async-start | bytes 12582912 | tf_op jit(solution)/shard_map/all_to_all | solution.py:87
Sparse Core Ops, SparseCore 0:
  9.8 77.3 all-gather.3
  89.0 73.0 all-gather.5
  163.9 73.0 all-gather.7
where the time goes:
time: 420 us; the launch traced here: 415 us
  waiting for transfers between devices  204 us (49%)
  local copies, waits for them, and re-layouts  101 us (24%)
  other arithmetic  42.2 us (10%)
  matrix products  30.7 us (7%)
  starting transfers between devices  23.3 us (6%)
  between operations  14.2 us (3%)
    all_to_all x1, waiting for transfers between devices, shards(): lax.all_to_all(outgoing, 'expert', split_axis=0, concat_axis=0, tiled=True)  86.7 us
    all_to_all x1, waiting for transfers between devices, shards(): lax.all_to_all(returning, 'expert', split_axis=0, concat_axis=0, tiled=True)  86.3 us
    gather x1, other arithmetic, shards(): priority[owner_tok]  30.2 us
    all_gather x1, waiting for transfers between devices, shards(): down_piece = lax.all_gather(w_down, 'dp', axis=1, tiled=True)  28.7 us
    scatter x1, local copies, waits for them, and re-layouts, shards(): outgoing = jnp.zeros((expert_count * slot_count, 2 * feat_width), jnp.bfl...  17.9 us
    gather x1, local copies, waits for them, and re-layouts, shards(): landed[target].reshape(tok_count, TOP, 2, feat_width).astype(jnp.float32)  17.7 us
    convert_element_type x1, local copies, waits for them, and re-layouts, shards(): returning = jnp.einsum('ecsm,ercd->semrd', placing, out_bf, preferred_ele...  14 us
    reshape x1, local copies, waits for them, and re-layouts, shards(): arrived.reshape(peer_count, local_count, slot_count, 2, feat_width)  11.5 us
  transfers between devices with their start and end apart: 6, of which 3 were waited for; matrix products, arithmetic and copies ran while one was open for 23% of the time, Pallas kernels for 0%

commit v1 on v0

--- a/solution.py
+++ b/solution.py
@@ -74,7 +74,9 @@
     ).astype(jnp.bfloat16)
     gate_piece = lax.all_gather(w_gate, "dp", axis=1, tiled=True)
     up_piece = lax.all_gather(w_up, "dp", axis=1, tiled=True)
-    down_piece = lax.all_gather(w_down, "dp", axis=1, tiled=True)
+    down_piece = jnp.concatenate(
+        lax.all_to_all(jnp.stack([w_down] * lax.axis_size("dp")), "dp", 0, 0), axis=1
+    )
     hidden = hidden_units(packed, gate_piece, up_piece)
     expert_out = jnp.einsum(
         "ercf,efd->ercd", hidden, down_piece, preferred_element_type=jnp.float32

time: 420 us -> 512 us (1.22)
  waiting for transfers between devices: 204 us -> 281 us
  local copies, waits for them, and re-layouts: 101 us -> 109 us
  starting transfers between devices: 23.3 us -> 29.6 us
    all_to_all x0 -> x1, waiting for transfers between devices: none -> 106 us  [shards(): lax.all_to_all(jnp.stack([w_down] * lax.axis_size('dp')), 'dp', 0, 0)]
    all_gather x1 -> x0, waiting for transfers between devices: 28.7 us -> none  [shards(): down_piece = lax.all_gather(w_down, 'dp', axis=1, tiled=True)]
    all_to_all x0 -> x1, starting transfers between devices: none -> 8.73 us  [shards(): lax.all_to_all(jnp.stack([w_down] * lax.axis_size('dp')), 'dp', 0, 0)]
    all_to_all x0 -> x1, local copies, waits for them, and re-layouts: none -> 6.57 us  [shards(): lax.all_to_all(jnp.stack([w_down] * lax.axis_size('dp')), 'dp', 0, 0)]
    dot_general x1, matrix products: 2.52 us -> 8.34 us  [shards(): jnp.einsum('ecsm,ercd->semrd', placing, out_bf, preferred_element_type=jn...]
    dot_general x1 -> x0, matrix products: 5.77 us -> none  [shards(): jnp.einsum('ercf,efd->ercd', hidden, down_piece, preferred_element_type=j...]
  transfers between devices with their start and end apart: 6 -> 6, of which waited for: 3 -> 3; matrix products, arithmetic and copies ran while one was open for 23% -> 20% of each run, Pallas kernels for 0% -> 0%
where the time goes in v1:
time: 512 us; the launch traced here: 507 us
  waiting for transfers between devices  281 us (55%)
  local copies, waits for them, and re-layouts  109 us (21%)
  other arithmetic  42.8 us (8%)
  matrix products  30.6 us (6%)
  starting transfers between devices  29.6 us (6%)
  between operations  14.5 us (3%)
    all_to_all x1, waiting for transfers between devices, shards(): lax.all_to_all(jnp.stack([w_down] * lax.axis_size('dp')), 'dp', 0, 0)  106 us
    all_to_all x1, waiting for transfers between devices, shards(): lax.all_to_all(outgoing, 'expert', split_axis=0, concat_axis=0, tiled=True)  86.8 us
    all_to_all x1, waiting for transfers between devices, shards(): lax.all_to_all(returning, 'expert', split_axis=0, concat_axis=0, tiled=True)  86.2 us
    gather x1, other arithmetic, shards(): priority[owner_tok]  30 us
    scatter x1, local copies, waits for them, and re-layouts, shards(): outgoing = jnp.zeros((expert_count * slot_count, 2 * feat_width), jnp.bfl...  17.8 us
    gather x1, local copies, waits for them, and re-layouts, shards(): landed[target].reshape(tok_count, TOP, 2, feat_width).astype(jnp.float32)  17.7 us
    convert_element_type x1, local copies, waits for them, and re-layouts, shards(): returning = jnp.einsum('ecsm,ercd->semrd', placing, out_bf, preferred_ele...  12.7 us
    reshape x1, local copies, waits for them, and re-layouts, shards(): arrived.reshape(peer_count, local_count, slot_count, 2, feat_width)  11.2 us
  transfers between devices with their start and end apart: 6, of which 3 were waited for; matrix products, arithmetic and copies ran while one was open for 20% of the time, Pallas kernels for 0%

profile of v1, /device:TPU:8, one launch (start us, length us, event | category | flops | bytes accessed | tf_op | source)
XLA Modules:
  0.0 507.5 jit_solution(11513106082147393432)
XLA Ops:
  7.2 0.7 all-gather.5.cloned.1.call-update
  7.9 0.8 copy.38
  8.7 0.1 eq.53
  8.9 0.9 reduce-window.6
  9.8 0.2 slice_reduce_fusion
  10.1 0.7 broadcast_multiply_fusion
  10.8 0.1 mul.102
  11.0 0.1 fusion.36
  11.1 1.7 fusion.47
  12.8 2.1 fusion.45
  14.9 2.1 fusion.46
  16.9 30.0 %select_select_fusion = s32[384]{0:T(512)S(1)} fusion(s32[384]{0:T(512)S(1)} %fusion.41, s32[]{:T(128)} %bitcast.2, s32[]{:T(128)} %bitcast.3, s32[]{:T(128)} %bitcast.4, s32[]{:T(128)} %bitcast.5, s32[]{:T(128)} %bitcast.6, s32[]{:T(128)} %bitcast.7, s32[]{:T(128)} %bitcast.8, s32[]{:T(128)} %bitcast.9, s32[]{:T(128)} %bitcast.10, s32[]{:T(128)} %bitcast.11, ...), kind=kLoop, calls=%fused_computation.70 | loop fusion | flops 36096 | bytes 3264 | tf_op jit(solution)/shard_map/gather | solution.py:50
  46.9 2.9 scatter_custom_fusion.1
  49.9 0.7 all_to_all.16
  50.5 8.2 %all-to-all-start.1 = ((s32[32,1,24]{2,1,0:T(1,128)}), s32[32,1,24]{2,1,0:T(1,128)S(1)}, u32[]{:S(2)}, u32[]{:S(2)}) async-start(s32[32,1,24]{2,1,0:T(1,128)} %bitcast.50), calls=%async_computation.1 | async-start | bytes 32768 | tf_op jit(solution)/shard_map/all_to_all | solution.py:56
  58.7 1.1 pad_maximum_fusion
  59.8 17.8 %scatter_custom_fusion = bf16[768,4096]{1,0:T(8,128)(2,1)} fusion(s32[384]{0:T(512)S(1)} %fusion.40, bf16[48,4096]{1,0:T(8,128)(2,1)S(1)} %pad_maximum_fusion, s32[1024]{0:T(1024)S(1)} %pad_clamp_fusion.1, bf16[]{:T(256)} %constant.15.clone.1), kind=kCustom, calls=%fused_computation.20 | custom fusion | bytes 6291458 | tf_op jit(solution)/shard_map/scatter | solution.py:45
  77.6 7.6 %all-to-all-start = ((bf16[32,24,4096]{2,1,0:T(8,128)(2,1)}), bf16[32,24,4096]{2,1,0:T(8,128)(2,1)}, u32[]{:S(2)}, u32[]{:S(2)}) async-start(bf16[32,24,4096]{2,1,0:T(8,128)(2,1)} %bitcast.134), calls=%async_computation | async-start | bytes 12582912 | tf_op jit(solution)/shard_map/all_to_all | solution.py:55
  85.2 0.7 all-gather.3.cloned.1.call-update
  85.9 86.8 %all-to-all-done = bf16[32,24,4096]{2,1,0:T(8,128)(2,1)} async-done(((bf16[32,24,4096]{2,1,0:T(8,128)(2,1)}), bf16[32,24,4096]{2,1,0:T(8,128)(2,1)}, u32[]{:S(2)}, u32[]{:S(2)}) %all-to-all-start) | async-done | bytes 6291488 | tf_op jit(solution)/shard_map/all_to_all | solution.py:55
  172.8 3.4 stack.6
  176.2 8.7 %all-to-all-start.2 = ((bf16[8,2,96,2048]{3,2,1,0:T(8,128)(2,1)}), bf16[8,2,96,2048]{3,2,1,0:T(8,128)(2,1)}, u32[]{:S(2)}, u32[]{:S(2)}) async-start(bf16[8,2,96,2048]{3,2,1,0:T(8,128)(2,1)} %stack.6), calls=%async_computation.2 | async-start | bytes 12582912 | tf_op jit(solution)/shard_map/all_to_all | solution.py:78
  185.0 0.1 copy.45
  185.1 0.1 reshape.206
  185.2 0.3 convert_reduce_fusion
  185.5 0.1 reduce_sum.81
  185.7 11.2 %reshape.204 = bf16[32,2,12,2,2048]{4,3,2,1,0:T(2,128)(2,1)} reshape(bf16[32,24,4096]{2,1,0:T(8,128)(2,1)} %all-to-all-done) | data formatting | bytes 12582912 | tf_op jit(solution)/shard_map/reshape | solution.py:58
  196.9 8.9 %bitcast_convert_fusion = bf16[2,2,2048,192]{2,3,1,0:T(8,128)(2,1)} fusion(bf16[32,2,12,2,2048]{4,3,2,1,0:T(2,128)(2,1)} %reshape.204, s32[2,32,12]{1,2,0:T(8,128)S(1)} %copy.46, pred[2,32,12]{1,2,0:T(8,128)(4,1)S(1)} %compare_and_fusion), kind=kOutput, calls=%fused_computation.8 | convolution fusion | flops 1209827328 | bytes 9441024 | tf_op jit(solution)/shard_map/ecsm,semrd->ercd/dot_general | solution.py:72
  205.8 6.4 %fusion = f32[2,2,192,768]{3,2,1,0:T(8,128)S(1)} fusion(bf16[2,768,2048]{2,1,0:T(8,128)(2,1)} %all-gather.5.cloned.1.call-done, bf16[2,2,2048,192]{2,3,1,0:T(8,128)(2,1)} %bitcast_convert_fusion), kind=kOutput, calls=%fused_computation.4 | convolution fusion | flops 2415919104 | bytes 11796480 | tf_op jit(solution)/shard_map/ercd,efd->ercf/dot_general | solution.py:13
  212.2 6.4 %fusion.2 = f32[2,2,192,768]{3,2,1,0:T(8,128)S(1)} fusion(bf16[2,768,2048]{2,1,0:T(8,128)(2,1)} %all-gather.3.cloned.1.call-done, bf16[2,2,2048,192]{2,3,1,0:T(8,128)(2,1)} %bitcast_convert_fusion), kind=kOutput, calls=%fused_computation.6 | convolution fusion | flops 2415919104 | bytes 11796480 | tf_op jit(solution)/shard_map/ercd,efd->ercf/dot_general | solution.py:12
  218.6 1.5 multiply_convert_fusion
  220.1 106.1 %all-to-all-done.2 = bf16[8,2,96,2048]{3,2,1,0:T(8,128)(2,1)} async-done(((bf16[8,2,96,2048]{3,2,1,0:T(8,128)(2,1)}), bf16[8,2,96,2048]{3,2,1,0:T(8,128)(2,1)}, u32[]{:S(2)}, u32[]{:S(2)}) %all-to-all-start.2) | async-done | bytes 6291488 | tf_op jit(solution)/shard_map/all_to_all | solution.py:78
  326.2 6.6 %copy.49 = bf16[8,2,96,2048]{3,2,0,1:T(8,128)(2,1)} copy(bf16[8,2,96,2048]{3,2,1,0:T(8,128)(2,1)} %all-to-all-done.2) | data formatting | bytes 12582912 | tf_op jit(solution)/shard_map/all_to_all | solution.py:78
  332.7 8.3 %convert_bitcast_fusion = bf16[32,2,12,2,2048]{4,0,2,3,1:T(8,128)(2,1)} fusion(bf16[2,768,2048,1]{2,1,3,0:T(8,128)(2,1)} %bitcast.135, bf16[2,1,192,768]{3,2,1,0:T(8,128)(2,1)S(1)} %copy-done.4, bf16[2,1,192,768]{3,2,1,0:T(8,128)(2,1)S(1)} %get-tuple-element.8, s32[2,32,12]{1,2,0:T(8,128)S(1)} %copy.46, pred[2,32,12]{1,2,0:T(8,128)(4,1)S(1)} %compare_and_fusion), kind=kOutput, calls=%fused_computation.11 | convolution fusion | flops 3629481984 | bytes 13766400 | tf_op jit(solution)/shard_map/ecsm,ercd->semrd/dot_general | solution.py:85
  341.1 12.7 %copy.50 = bf16[32,2,12,2,2048]{4,3,2,1,0:T(2,128)(2,1)} copy(bf16[32,2,12,2,2048]{4,0,2,3,1:T(8,128)(2,1)} %convert_bitcast_fusion) | data formatting | bytes 12582912 | tf_op jit(solution)/shard_map/convert_element_type | solution.py:87
  353.8 11.1 %reshape.209 = bf16[32,24,4096]{2,1,0:T(8,128)(2,1)} reshape(bf16[32,2,12,2,2048]{4,3,2,1,0:T(2,128)(2,1)} %copy.50) | data formatting | bytes 12582912 | tf_op jit(solution)/shard_map/reshape | solution.py:88
  364.9 5.1 %all-to-all-start.3 = ((bf16[32,24,4096]{2,1,0:T(8,128)(2,1)}), bf16[32,24,4096]{2,1,0:T(8,128)(2,1)}, u32[]{:S(2)}, u32[]{:S(2)}) async-start(bf16[32,24,4096]{2,1,0:T(8,128)(2,1)} %reshape.209), calls=%async_computation.3 | async-start | bytes 12582912 | tf_op jit(solution)/shard_map/all_to_all | solution.py:89
  370.0 0.2 fusion.49
  370.3 0.2 fusion.48
  370.5 0.2 convolution_add_fusion
  370.7 0.2 multiply_reduce_fusion.1
  371.0 0.1 exponential_reduce_fusion
  371.1 0.2 multiply_reduce_fusion.3
  371.3 86.2 %all-to-all-done.3 = bf16[32,24,4096]{2,1,0:T(8,128)(2,1)} async-done(((bf16[32,24,4096]{2,1,0:T(8,128)(2,1)}), bf16[32,24,4096]{2,1,0:T(8,128)(2,1)}, u32[]{:S(2)}, u32[]{:S(2)}) %all-to-all-start.3) | async-done | bytes 6291488 | tf_op jit(solution)/shard_map/all_to_all | solution.py:89
  457.6 11.1 %reshape.210 = bf16[768,2,2048]{2,1,0:T(2,128)(2,1)} reshape(bf16[32,24,4096]{2,1,0:T(8,128)(2,1)} %all-to-all-done.3) | data formatting | bytes 12582912 | tf_op jit(solution)/shard_map/reshape | solution.py:90
  468.7 17.7 %gather_fusion = bf16[384,2,2048]{2,1,0:T(2,128)(2,1)S(1)} fusion(bf16[768,2,2048]{2,1,0:T(2,128)(2,1)} %reshape.210, s32[1024]{0:T(1024)S(1)} %pad_clamp_fusion), kind=kCustom, calls=%fused_computation.1 | custom fusion | bytes 6292992 | tf_op jit(solution)/shard_map/gather | solution.py:91
  486.4 6.5 %fusion.44 = (f32[48,8,1,2048]{3,2,1,0:T(1,128)S(1)}, f32[48,8,1,2048]{3,2,1,0:T(1,128)}) fusion(bf16[48,8,2,2048]{3,2,1,0:T(2,128)(2,1)S(1)} %bitcast.133), kind=kLoop, calls=%fused_computation.78 | loop fusion | bytes 12582912 | tf_op jit(solution)/shard_map/slice | solution.py:102
  492.9 7.5 %fusion.9 = (bf16[48,2048]{1,0:T(8,128)(2,1)}, bf16[48,2048]{1,0:T(8,128)(2,1)}) fusion(f32[48,8,1,2048]{3,2,1,0:T(1,128)} %get-tuple-element.11, f32[48,8,1,2048]{3,2,1,0:T(1,128)S(1)} %get-tuple-element.10, f32[48,8]{1,0:T(8,128)S(1)} %subtract_multiply_fusion, f32[48,8]{1,0:T(8,128)S(1)} %get-tuple-element.7), kind=kLoop, calls=%fused_computation.16 | loop fusion | flops 4521984 | bytes 6687744 | tf_op jit(solution)/shard_map/reduce_sum | solution.py:103
  (31 shorter events, 0.7 us)
Async XLA Ops:
  7.2 362.9 %copy-start = (bf16[2048,64]{0,1:T(8,128)(2,1)S(1)}, bf16[2048,64]{0,1:T(8,128)(2,1)}, u32[]{:S(2)}) copy-start(bf16[2048,64]{0,1:T(8,128)(2,1)} %param.11) | copy-start | bytes 786436
  7.2 198.7 %all-gather.5.cloned.1.call-start = ((), (), s32[]{:S(2)}) async-start(), calls=%async_computation.5 | async-start | bytes 7077888 | tf_op jit(solution)/shard_map/all_gather | solution.py:76
  50.5 27.1 %all-to-all-start.1 = ((s32[32,1,24]{2,1,0:T(1,128)}), s32[32,1,24]{2,1,0:T(1,128)S(1)}, u32[]{:S(2)}, u32[]{:S(2)}) async-start(s32[32,1,24]{2,1,0:T(1,128)} %bitcast.50), calls=%async_computation.1 | async-start | bytes 32768 | tf_op jit(solution)/shard_map/all_to_all | solution.py:56
  77.6 95.2 %copy-start.2 = (bf16[2,96,2048]{2,1,0:T(8,128)(2,1)S(1)}, bf16[2,96,2048]{2,1,0:T(8,128)(2,1)}, u32[]{:S(2)}) copy-start(bf16[2,96,2048]{2,1,0:T(8,128)(2,1)} %param.17) | copy-start | bytes 2359300
  77.6 95.2 %all-to-all-start = ((bf16[32,24,4096]{2,1,0:T(8,128)(2,1)}), bf16[32,24,4096]{2,1,0:T(8,128)(2,1)}, u32[]{:S(2)}, u32[]{:S(2)}) async-start(bf16[32,24,4096]{2,1,0:T(8,128)(2,1)} %bitcast.134), calls=%async_computation | async-start | bytes 12582912 | tf_op jit(solution)/shard_map/all_to_all | solution.py:55
  85.2 127.1 %all-gather.3.cloned.1.call-start = ((), (), s32[]{:S(2)}) async-start(), calls=%async_computation.4 | async-start | bytes 7077888 | tf_op jit(solution)/shard_map/all_gather | solution.py:75
  176.2 150.0 %all-to-all-start.2 = ((bf16[8,2,96,2048]{3,2,1,0:T(8,128)(2,1)}), bf16[8,2,96,2048]{3,2,1,0:T(8,128)(2,1)}, u32[]{:S(2)}, u32[]{:S(2)}) async-start(bf16[8,2,96,2048]{3,2,1,0:T(8,128)(2,1)} %stack.6), calls=%async_computation.2 | async-start | bytes 12582912 | tf_op jit(solution)/shard_map/all_to_all | solution.py:78
  220.1 112.6 %copy-start.4 = (bf16[2,1,192,768]{3,2,1,0:T(8,128)(2,1)S(1)}, bf16[2,1,192,768]{3,2,1,0:T(8,128)(2,1)}, u32[]{:S(2)}) copy-start(bf16[2,1,192,768]{3,2,1,0:T(8,128)(2,1)} %get-tuple-element.9) | copy-start | bytes 1769476
  364.9 5.1 %copy-start.3 = (bf16[48,2048]{1,0:T(8,128)(2,1)S(1)}, bf16[48,2048]{1,0:T(8,128)(2,1)}, u32[]{:S(2)}) copy-start(bf16[48,2048]{1,0:T(8,128)(2,1)} %param.10) | copy-start | bytes 589828
  364.9 5.4 %copy-start.1 = (bf16[48,2048]{1,0:T(8,128)(2,1)S(1)}, bf16[48,2048]{1,0:T(8,128)(2,1)}, u32[]{:S(2)}) copy-start(bf16[48,2048]{1,0:T(8,128)(2,1)} %param.9) | copy-start | bytes 589828
  364.9 5.6 %copy-start.5 = (bf16[2048,64]{0,1:T(8,128)(2,1)S(1)}, bf16[2048,64]{0,1:T(8,128)(2,1)}, u32[]{:S(2)}) copy-start(bf16[2048,64]{0,1:T(8,128)(2,1)} %param.12) | copy-start | bytes 786436
  364.9 92.7 %all-to-all-start.3 = ((bf16[32,24,4096]{2,1,0:T(8,128)(2,1)}), bf16[32,24,4096]{2,1,0:T(8,128)(2,1)}, u32[]{:S(2)}, u32[]{:S(2)}) async-start(bf16[32,24,4096]{2,1,0:T(8,128)(2,1)} %reshape.209), calls=%async_computation.3 | async-start | bytes 12582912 | tf_op jit(solution)/shard_map/all_to_all | solution.py:89
Sparse Core Ops, SparseCore 0:
  9.8 77.3 all-gather.4
  89.0 76.0 all-gather.2
